TPU v7x, 512 devices: a whole 4x4x16 slice. The times are simulated.
512 devices in a mesh: span: 8 (over z_hi, y), stream: 64 (over x, z_lo, core).
Axes of the slice: x: 4, y: 4, z: 16 (z_hi: 2, z_lo: 8; z = z_hi * 8 + z_lo), core: 2. Of those that a mesh axis runs over, the one named last changes fastest.
Arguments:
- velocity: float32 [3, 32, 512, 256], P(None, 'span', 'stream'), may hold values from -32 to 32
- strain: float32 [6, 32, 512, 256], P(None, 'span', 'stream'), may hold values from -4 to 4
- row_bins: int32 [512], P('stream'), may hold values from 0 to 63, never falling along the last dimension, each value on 1 to 16 neighbouring positions
- cotangent: float32 [6, 32, 512, 256], P(None, 'span', 'stream'), may hold values from -6 to 6
Outputs:
- model_residual: float32 [6, 32, 512, 256], P(None, 'span', 'stream')
- velocity_grad: float32 [3, 32, 512, 256], P(None, 'span', 'stream')
Inputs may be any that keep to these rules, and one draw needn't show every extreme that they name: `row_bins`: bins never fall along the rows, and every bin holds 1 to 16 rows.
All inputs are finite; a program needn't handle non-finite values.
Results may differ from a plain program's by a relative error of at most 0.0003.
Values sent between devices are 32-bit elements; how exact they have to be, the bound alone decides.
A program may use at most 64 MiB of HBM per device.

v0:
```python
import jax
import jax.numpy as jnp
import numpy as np
from jax import lax
from jax.sharding import PartitionSpec as P

NBINS = 64
FILTER_ALPHA = 0.45
CENTER_WEIGHT = 0.95
SIDE_WEIGHT = 0.475
STRAIN_FLOOR = 0.25
EPSILON = 1e-06
INDEX_PAIRS = ((0, 0), (0, 1), (0, 2), (1, 1), (1, 2), (2, 2))
PAIR_WEIGHTS = (1.0, 2.0, 2.0, 1.0, 2.0, 1.0)
HIGHEST = lax.Precision.HIGHEST


def extended(array, sides, width):
    for axis, dim in sides:
        peers, length = (lax.axis_size(axis), array.shape[dim])
        up = [(i, (i + 1) % peers) for i in range(peers)]
        down = [(j, i) for i, j in up]
        last = lax.slice_in_dim(array, length - width, length, axis=dim)
        first = lax.slice_in_dim(array, 0, width, axis=dim)
        before = lax.ppermute(last, axis, up)
        after = lax.ppermute(first, axis, down)
        array = jnp.concatenate([before, array, after], axis=dim)
    return array


def invert_table(matrix):
    extent = matrix.shape[0]
    augmented = np.concatenate([np.array(matrix), np.eye(extent)], axis=1)
    for column in range(extent):
        pivot_row = column + int(np.argmax(np.abs(augmented[column:, column])))
        swapped = augmented[[pivot_row, column]]
        augmented[[column, pivot_row]] = swapped
        augmented[column] = augmented[column] / augmented[column, column]
        for row_index in range(extent):
            if row_index != column:
                augmented[row_index] = (
                    augmented[row_index] - augmented[row_index, column] * augmented[column]
                )
    return augmented[:, extent:]


def loop_tables(cell_count, devices):
    local_system = np.eye(cell_count) + FILTER_ALPHA * (
        np.eye(cell_count, k=1) + np.eye(cell_count, k=-1)
    )
    local_inverse = invert_table(local_system)
    first_column = local_inverse[:, 0]
    last_column = local_inverse[:, cell_count - 1]
    unknowns = 2 * devices
    coupling = np.eye(unknowns)
    for device in range(devices):
        previous = (device - 1) % devices
        following = (device + 1) % devices
        for which_end, cell_index in ((0, 0), (1, cell_count - 1)):
            target = 2 * device + which_end
            coupling[target, 2 * previous + 1] += FILTER_ALPHA * first_column[cell_index]
            coupling[target, 2 * following] += FILTER_ALPHA * last_column[cell_index]
    reduced = invert_table(coupling)
    selectors = np.stack(
        [
            reduced[[2 * ((device - 1) % devices) + 1, 2 * ((device + 1) % devices)], :]
            for device in range(devices)
        ]
    )
    return (
        jnp.asarray(local_inverse, jnp.float32),
        jnp.asarray(first_column, jnp.float32),
        jnp.asarray(last_column, jnp.float32),
        jnp.asarray(selectors, jnp.float32),
    )


def rim_side(values):
    padded = extended(values, (("span", 1),), 1)
    return CENTER_WEIGHT * values + SIDE_WEIGHT * (padded[:, 2:] + padded[:, :-2])


def solve_loop(values, tables, own_index):
    local_inverse, first_column, last_column, selectors = tables
    particular = jnp.einsum("ij,fjyx->fiyx", local_inverse, values, precision=HIGHEST)
    end_values = jnp.stack([particular[:, 0], particular[:, -1]], axis=0)
    selector = lax.dynamic_index_in_dim(selectors, own_index, 0, keepdims=False)
    gathered_piece = lax.all_gather(end_values, "span", axis=0, tiled=True)
    columns = lax.slice_in_dim(selector, 0, gathered_piece.shape[0], axis=1)
    neighbours = jnp.zeros_like(end_values) + jnp.einsum(
        "ae,efyx->afyx", columns, gathered_piece, precision=HIGHEST
    )
    previous = neighbours[0]
    following = neighbours[1]
    solved = particular - FILTER_ALPHA * (
        first_column[None, :, None, None] * previous[:, None]
        + last_column[None, :, None, None] * following[:, None]
    )
    return (solved, previous, following)


def solve_back(values, tables, own_index):
    local_inverse, first_column, last_column, selectors = tables
    selector = lax.dynamic_index_in_dim(selectors, own_index, 0, keepdims=False)
    near_bar = -FILTER_ALPHA * jnp.stack(
        [
            jnp.einsum("i,fiyx->fyx", first_column, values, precision=HIGHEST),
            jnp.einsum("i,fiyx->fyx", last_column, values, precision=HIGHEST),
        ],
        axis=0,
    )
    columns = lax.slice_in_dim(selector, 0, 2 * lax.axis_size("span"), axis=1)
    end_bar = lax.psum_scatter(
        jnp.einsum("ae,afyx->efyx", columns, near_bar, precision=HIGHEST),
        "span",
        scatter_dimension=0,
        tiled=True,
    )
    particular_bar = values.at[:, 0].add(end_bar[0]).at[:, -1].add(end_bar[1])
    return jnp.einsum("ji,fjyx->fiyx", local_inverse, particular_bar, precision=HIGHEST)


def smooth(values, tables, own_index):
    return solve_loop(rim_side(values), tables, own_index)[0]


def unsmooth(values, tables, own_index):
    return rim_side(solve_back(values, tables, own_index))


def on_device(velocity, strain, row_bins, cotangent):
    tables = loop_tables(velocity.shape[1], lax.axis_size("span"))
    own_index = lax.axis_index("span")
    weights = jnp.asarray(PAIR_WEIGHTS, jnp.float32)[:, None, None, None]
    products = jnp.stack([velocity[former] * velocity[latter] for former, latter in INDEX_PAIRS])
    size_field = jnp.sqrt(
        jnp.maximum(2.0 * jnp.sum(weights * strain * strain, axis=0), STRAIN_FLOOR)
    )
    fields = jnp.concatenate([velocity, products, size_field[None]], axis=0)
    filtered = smooth(fields, tables, own_index)
    coarse = jnp.stack([filtered[former] * filtered[latter] for former, latter in INDEX_PAIRS])
    leonard = filtered[3:9] - coarse
    model_term = products - coarse + 2.0 * (4.0 * filtered[9] - size_field)[None] * strain
    onehot = (row_bins[:, None] == jnp.arange(NBINS, dtype=jnp.int32)[None, :]).astype(jnp.float32)
    cross_local = jnp.dot(
        jnp.sum(weights * leonard * model_term, axis=(0, 1, 3)), onehot, precision=HIGHEST
    )
    square_local = jnp.dot(
        jnp.sum(weights * model_term * model_term, axis=(0, 1, 3)), onehot, precision=HIGHEST
    )
    blame_local = jnp.dot(
        jnp.sum(cotangent * model_term, axis=(0, 1, 3)), onehot, precision=HIGHEST
    )
    cross_bins, square_bins, blame_bins = lax.psum(
        (cross_local, square_local, blame_local), ("span", "stream")
    )
    denominator = square_bins + EPSILON
    coefficient = cross_bins / denominator
    row_coefficient = jnp.dot(onehot, coefficient, precision=HIGHEST)[None, None, :, None]
    residual = leonard - row_coefficient * model_term
    coefficient_bar = -blame_bins
    cross_bar = coefficient_bar / denominator
    square_bar = -coefficient_bar * coefficient / denominator
    row_cross = jnp.dot(onehot, cross_bar, precision=HIGHEST)[None, None, :, None]
    row_square = jnp.dot(onehot, square_bar, precision=HIGHEST)[None, None, :, None]
    leonard_bar = cotangent + row_cross * weights * model_term
    model_bar = (
        -row_coefficient * cotangent
        + row_cross * weights * leonard
        + 2.0 * row_square * weights * model_term
    )
    zero_field = jnp.zeros_like(velocity[0])
    coarse_bar = [zero_field, zero_field, zero_field]
    for position, (former, latter) in enumerate(INDEX_PAIRS):
        combined = leonard_bar[position] + model_bar[position]
        coarse_bar[former] = coarse_bar[former] - combined * filtered[latter]
        coarse_bar[latter] = coarse_bar[latter] - combined * filtered[former]
    pulled = unsmooth(
        jnp.concatenate([jnp.stack(coarse_bar), leonard_bar], axis=0), tables, own_index
    )
    gradient_parts = [pulled[0], pulled[1], pulled[2]]
    for position, (former, latter) in enumerate(INDEX_PAIRS):
        through = pulled[3 + position] + model_bar[position]
        gradient_parts[former] = gradient_parts[former] + through * velocity[latter]
        gradient_parts[latter] = gradient_parts[latter] + through * velocity[former]
    return (residual, jnp.stack(gradient_parts))


def solution(mesh):
    return jax.shard_map(
        on_device,
        mesh=mesh,
        in_specs=(
            P(None, "span", "stream", None),
            P(None, "span", "stream", None),
            P("stream"),
            P(None, "span", "stream", None),
        ),
        out_specs=(P(None, "span", "stream", None), P(None, "span", "stream", None)),
        check_vma=False,
    )
```

profile of v0, /device:TPU:130, one launch (start us, length us, event | category | flops | bytes accessed | tf_op | source)
XLA Modules:
  0.0 400.0 jit_solution(6443093883510731724)
XLA Ops:
  7.2 0.8 fusion.61
  8.0 0.9 constant_dynamic-update-slice_fusion.7
  8.9 1.1 fusion.10
  10.4 13.4 %collective-permute-start = (f32[10,1,8,256]{3,2,1,0:T(8,128)S(1)}, f32[10,1,8,256]{3,2,1,0:T(8,128)S(1)}, u32[]{:S(2)}, u32[]{:S(2)}) collective-permute-start(f32[10,1,8,256]{3,2,1,0:T(8,128)S(1)} %get-tuple-element.54), channel_id=1, source_target_pairs={{64,0},{128,64},{192,128},{256,192},{320,256},{384,320},{448,384},... | collective-permute-start | bytes 245768 | tf_op jit(solution)/shard_map/ppermute | solution.py:26
  23.7 1.9 collective-permute-start.1
  25.7 0.1 collective-permute-done
  25.8 16.1 %collective-permute-done.1 = f32[10,1,8,256]{3,2,1,0:T(8,128)S(1)} collective-permute-done((f32[10,1,8,256]{3,2,1,0:T(8,128)S(1)}, f32[10,1,8,256]{3,2,1,0:T(8,128)S(1)}, u32[]{:S(2)}, u32[]{:S(2)}) %collective-permute-start.1) | collective-permute-done | bytes 81952 | tf_op jit(solution)/shard_map/ppermute | solution.py:25
  42.0 0.7 convolution_bitcast_fusion
  42.7 0.1 slice_bitcast_fusion.1
  42.9 0.2 pad_maximum_fusion.5
  43.0 0.7 copy.44
  43.8 84.5 %all-gather.2.cloned.1.call-done = f32[16,10,8,256]{3,2,1,0:T(8,128)} async-done(((f32[2,10,8,256]{3,2,1,0:T(8,128)}), f32[16,10,8,256]{3,2,1,0:T(8,128)}) %all-gather.2.cloned.1.call-update) | async-done | bytes 1310736 | tf_op jit(solution)/shard_map/all_gather | solution.py:88
  128.3 2.7 fusion
  131.1 0.1 fusion.59
  131.2 0.2 multiply_subtract_fusion
  131.6 0.3 copy-done
  132.0 0.1 copy-done.1
  132.1 0.4 fusion.11
  132.5 0.2 convolution_bitcast_fusion.6
  132.6 0.2 convolution_bitcast_fusion.7
  132.8 0.2 convolution_bitcast_fusion.4
  133.0 107.1 %all-reduce = (f32[64]{0:T(128)S(1)}, f32[64]{0:T(128)S(1)}, f32[64]{0:T(128)S(1)}) all-reduce(f32[64]{0:T(128)S(1)} %convolution_bitcast_fusion.7, f32[64]{0:T(128)S(1)} %convolution_bitcast_fusion.6, f32[64]{0:T(128)S(1)} %convolution_bitcast_fusion.4), channel_id=1, replica_groups=mesh['span'=8,'stream'=64] {'span','stream'}, use_global_device_ids=true, to_apply=%region_2.3 | all-reduce | flops 192 | bytes 1536 | tf_op jit(solution)/shard_map/psum | solution.py:154
  240.1 0.2 convolution_bitcast_fusion.3
  240.3 0.2 fusion.2
  240.5 0.2 fusion.62
  240.7 0.1 broadcast_multiply_fusion
  240.7 0.2 multiply_add_fusion
  241.1 0.1 pad_maximum_fusion.4
  241.2 0.2 copy-done.5
  241.4 0.6 fusion.64
  242.1 0.6 fusion.63
  242.8 1.9 fusion.12
  244.8 1.7 copy.50
  246.5 108.7 %reduce-scatter.2.cloned.1.call-done = f32[2,9,8,256]{3,2,1,0:T(8,128)} async-done(((f32[16,9,8,256]{3,2,1,0:T(8,128)}), f32[2,9,8,256]{3,2,1,0:T(8,128)}) %reduce-scatter.2.cloned.1.call-update) | async-done | bytes 147472 | tf_op jit(solution)/shard_map/reduce_scatter | solution.py:113
  355.2 0.9 fusion.60
  356.1 0.1 slice_add_fusion.1
  356.3 2.2 scatter-add.6
  358.4 0.1 slice_add_fusion
  358.6 2.2 scatter-add.9
  360.7 0.7 convolution_bitcast_fusion.1
  361.4 0.1 fusion.58
  361.5 12.4 %collective-permute-start.2 = (f32[9,1,8,256]{3,1,2,0:T(1,128)S(1)}, f32[9,1,8,256]{3,1,2,0:T(1,128)S(1)}, u32[]{:S(2)}, u32[]{:S(2)}) collective-permute-start(f32[9,1,8,256]{3,1,2,0:T(1,128)S(1)} %get-tuple-element.56), channel_id=1, source_target_pairs={{64,0},{128,64},{192,128},{256,192},{320,256},{384,320},{448,384},... | collective-permute-start | bytes 221192 | tf_op jit(solution)/shard_map/ppermute | solution.py:26
  373.9 1.9 collective-permute-start.3
  375.9 0.7 copy.54
  376.6 15.4 %collective-permute-done.3 = f32[9,1,8,256]{3,1,2,0:T(1,128)S(1)} collective-permute-done((f32[9,1,8,256]{3,1,2,0:T(1,128)S(1)}, f32[9,1,8,256]{3,1,2,0:T(1,128)S(1)}, u32[]{:S(2)}, u32[]{:S(2)}) %collective-permute-start.3) | collective-permute-done | bytes 73760 | tf_op jit(solution)/shard_map/ppermute | solution.py:25
  392.0 0.3 fusion.9
  392.4 0.1 fusion.20
  392.5 0.7 copy.55
  (52 shorter events, 1.0 us)
Async XLA Ops:
  7.2 121.1 %all-gather.2.cloned.1.call-start = ((), (), s32[]{:S(2)}) async-start(), calls=%async_computation.1 | async-start | bytes 1474560 | tf_op jit(solution)/shard_map/all_gather | solution.py:88
  8.9 33.1 %copy-start.2 = (f32[4,4,1,1]{1,0,3,2:T(4,128)S(1)}, f32[4,4,1,1]{1,0,3,2:T(4,128)}, u32[]{:S(2)}) copy-start(f32[4,4,1,1]{1,0,3,2:T(4,128)} %constant.110) | copy-start | bytes 196
  10.4 15.4 %collective-permute-start = (f32[10,1,8,256]{3,2,1,0:T(8,128)S(1)}, f32[10,1,8,256]{3,2,1,0:T(8,128)S(1)}, u32[]{:S(2)}, u32[]{:S(2)}) collective-permute-start(f32[10,1,8,256]{3,2,1,0:T(8,128)S(1)} %get-tuple-element.54), channel_id=1, source_target_pairs={{64,0},{128,64},{192,128},{256,192},{320,256},{384,320},{448,384},... | collective-permute-start | bytes 245768 | tf_op jit(solution)/shard_map/ppermute | solution.py:26
  23.7 18.2 %collective-permute-start.1 = (f32[10,1,8,256]{3,2,1,0:T(8,128)S(1)}, f32[10,1,8,256]{3,2,1,0:T(8,128)S(1)}, u32[]{:S(2)}, u32[]{:S(2)}) collective-permute-start(f32[10,1,8,256]{3,2,1,0:T(8,128)S(1)} %get-tuple-element.55), channel_id=1, source_target_pairs={{0,64},{64,128},{128,192},{192,256},{256,320},{320,384},{384,448},... | collective-permute-start | bytes 245768 | tf_op jit(solution)/shard_map/ppermute | solution.py:25
  43.0 88.2 %copy-start.6 = (f32[4]{0:T(128)S(1)}, f32[4]{0:T(128)}, u32[]{:S(2)}) copy-start(f32[4]{0:T(128)} %constant.103.clone) | copy-start | bytes 52
  43.0 88.2 %copy-start.7 = (f32[4]{0:T(128)S(1)}, f32[4]{0:T(128)}, u32[]{:S(2)}) copy-start(f32[4]{0:T(128)} %constant.102.clone) | copy-start | bytes 52
  43.7 311.5 %reduce-scatter.2.cloned.1.call-start = ((), (), s32[]{:S(2)}) async-start(), calls=%async_computation.2 | async-start | bytes 1327104 | tf_op jit(solution)/shard_map/reduce_scatter | solution.py:113
  131.0 0.9 copy-start
  131.0 1.0 copy-start.1
  131.0 1.0 copy-start.3
  131.2 1.2 copy-start.8
  240.7 0.7 copy-start.5
  241.0 1.1 copy-start.4
  361.5 15.1 %collective-permute-start.2 = (f32[9,1,8,256]{3,1,2,0:T(1,128)S(1)}, f32[9,1,8,256]{3,1,2,0:T(1,128)S(1)}, u32[]{:S(2)}, u32[]{:S(2)}) collective-permute-start(f32[9,1,8,256]{3,1,2,0:T(1,128)S(1)} %get-tuple-element.56), channel_id=1, source_target_pairs={{64,0},{128,64},{192,128},{256,192},{320,256},{384,320},{448,384},... | collective-permute-start | bytes 221192 | tf_op jit(solution)/shard_map/ppermute | solution.py:26
  373.9 18.0 %collective-permute-start.3 = (f32[9,1,8,256]{3,1,2,0:T(1,128)S(1)}, f32[9,1,8,256]{3,1,2,0:T(1,128)S(1)}, u32[]{:S(2)}, u32[]{:S(2)}) collective-permute-start(f32[9,1,8,256]{3,1,2,0:T(1,128)S(1)} %get-tuple-element.57), channel_id=1, source_target_pairs={{0,64},{64,128},{128,192},{192,256},{256,320},{320,384},{384,448},... | collective-permute-start | bytes 221192 | tf_op jit(solution)/shard_map/ppermute | solution.py:25
Sparse Core Ops, SparseCore 0:
  43.9 84.3 all-gather.1
  246.6 108.5 reduce-scatter.1
where the time goes:
time: 400 us
  waiting for transfers between devices  225 us (56%)
  blocking collectives  107 us (27%)
  starting transfers between devices  29.7 us (7%)
  between operations  14.5 us (4%)
  local copies, waits for them, and re-layouts  12 us (3%)
  matrix products  8.42 us (2%)
    reduce_scatter x1, waiting for transfers between devices, solve_back(): lax.psum_scatter(jnp.einsum('ae,afyx->efyx', columns, near_bar, precision...  109 us
    psum x1, blocking collectives, on_device(): lax.psum((cross_local, square_local, blame_local), ('span', 'stream'))  107 us
    all_gather x1, waiting for transfers between devices, solve_loop(): gathered_piece = lax.all_gather(end_values, 'span', axis=0, tiled=True)  84.5 us
    ppermute x2, waiting for transfers between devices, extended(): before = lax.ppermute(last, axis, up)  31.5 us
    ppermute x2, starting transfers between devices, extended(): after = lax.ppermute(first, axis, down)  25.8 us
  transfers between devices with their start and end apart: 6, of which 6 were waited for; matrix products, arithmetic and copies ran while one was open for 0% of the time, Pallas kernels for 0%

commit v1 on v0

--- a/solution.py
+++ b/solution.py
@@ -85,7 +85,9 @@
     particular = jnp.einsum("ij,fjyx->fiyx", local_inverse, values, precision=HIGHEST)
     end_values = jnp.stack([particular[:, 0], particular[:, -1]], axis=0)
     selector = lax.dynamic_index_in_dim(selectors, own_index, 0, keepdims=False)
-    gathered_piece = lax.all_gather(end_values, "span", axis=0, tiled=True)
+    gathered_piece = jnp.concatenate(
+        lax.all_to_all(jnp.stack([end_values] * lax.axis_size("span")), "span", 0, 0), axis=0
+    )
     columns = lax.slice_in_dim(selector, 0, gathered_piece.shape[0], axis=1)
     neighbours = jnp.zeros_like(end_values) + jnp.einsum(
         "ae,efyx->afyx", columns, gathered_piece, precision=HIGHEST

time: 400 us -> 386 us (0.965)
  the two profiles are of different devices: /device:TPU:130 before, /device:TPU:128 now
where the time goes in v1:
time: 386 us; the launch traced here: 385 us
  waiting for transfers between devices  195 us (51%)
  blocking collectives  117 us (30%)
  starting transfers between devices  34 us (9%)
  local copies, waits for them, and re-layouts  14.7 us (4%)
  between operations  14.5 us (4%)
  matrix products  7.11 us (2%)
    psum x1, blocking collectives, on_device(): lax.psum((cross_local, square_local, blame_local), ('span', 'stream'))  117 us
    reduce_scatter x1, waiting for transfers between devices, solve_back(): lax.psum_scatter(jnp.einsum('ae,afyx->efyx', columns, near_bar, precision...  110 us
    all_to_all x1, waiting for transfers between devices, solve_loop(): lax.all_to_all(jnp.stack([end_values] * lax.axis_size('span')), 'span', 0...  53 us
    ppermute x2, waiting for transfers between devices, extended(): before = lax.ppermute(last, axis, up)  31.3 us
    ppermute x2, starting transfers between devices, extended(): after = lax.ppermute(first, axis, down)  25.7 us
  transfers between devices with their start and end apart: 6, of which 6 were waited for; matrix products, arithmetic and copies ran while one was open for 0% of the time, Pallas kernels for 0%

profile of v1, /device:TPU:128, one launch (start us, length us, event | category | flops | bytes accessed | tf_op | source)
XLA Modules:
  0.0 385.4 jit_solution(17453425284992110512)
XLA Ops:
  7.2 0.8 fusion.60
  8.0 0.9 constant_dynamic-update-slice_fusion.7
  9.1 1.1 fusion.8
  10.3 13.4 %collective-permute-start = (f32[10,1,8,256]{3,2,1,0:T(8,128)S(1)}, f32[10,1,8,256]{3,2,1,0:T(8,128)S(1)}, u32[]{:S(2)}, u32[]{:S(2)}) collective-permute-start(f32[10,1,8,256]{3,2,1,0:T(8,128)S(1)} %get-tuple-element.54), channel_id=1, source_target_pairs={{64,0},{128,64},{192,128},{256,192},{320,256},{384,320},{448,384},... | collective-permute-start | bytes 245768 | tf_op jit(solution)/shard_map/ppermute | solution.py:26
  23.7 1.9 collective-permute-start.1
  25.6 0.1 collective-permute-done
  25.7 16.1 %collective-permute-done.1 = f32[10,1,8,256]{3,2,1,0:T(8,128)S(1)} collective-permute-done((f32[10,1,8,256]{3,2,1,0:T(8,128)S(1)}, f32[10,1,8,256]{3,2,1,0:T(8,128)S(1)}, u32[]{:S(2)}, u32[]{:S(2)}) %collective-permute-start.1) | collective-permute-done | bytes 81952 | tf_op jit(solution)/shard_map/ppermute | solution.py:25
  41.9 0.7 convolution_bitcast_fusion
  42.7 0.1 slice_bitcast_fusion.1
  42.8 0.2 pad_maximum_fusion.5
  43.0 1.7 stack.17
  44.7 4.3 %all-to-all-start = ((f32[8,2,10,8,256]{4,1,3,2,0:T(2,128)}), f32[8,2,10,8,256]{4,1,3,2,0:T(2,128)S(1)}, u32[]{:S(2)}, u32[]{:S(2)}) async-start(f32[8,2,10,8,256]{4,1,3,2,0:T(2,128)} %stack.17), calls=%async_computation | async-start | bytes 2621440 | tf_op jit(solution)/shard_map/all_to_all | solution.py:89
  49.1 53.0 %all-to-all-done = f32[8,2,10,8,256]{4,1,3,2,0:T(2,128)S(1)} async-done(((f32[8,2,10,8,256]{4,1,3,2,0:T(2,128)}), f32[8,2,10,8,256]{4,1,3,2,0:T(2,128)S(1)}, u32[]{:S(2)}, u32[]{:S(2)}) %all-to-all-start) | async-done | bytes 1310752 | tf_op jit(solution)/shard_map/all_to_all | solution.py:89
  102.1 0.7 copy.44
  102.8 0.9 reshape.166
  103.7 1.4 fusion.37
  105.2 0.1 fusion.58
  105.4 0.2 multiply_subtract_fusion
  105.8 0.3 copy-done
  106.2 0.4 fusion.9
  106.6 0.2 convolution_bitcast_fusion.4
  106.8 0.2 convolution_bitcast_fusion.6
  107.0 0.2 convolution_bitcast_fusion.7
  107.2 116.7 %all-reduce = (f32[64]{0:T(128)S(1)}, f32[64]{0:T(128)S(1)}, f32[64]{0:T(128)S(1)}) all-reduce(f32[64]{0:T(128)S(1)} %convolution_bitcast_fusion.7, f32[64]{0:T(128)S(1)} %convolution_bitcast_fusion.6, f32[64]{0:T(128)S(1)} %convolution_bitcast_fusion.4), channel_id=1, replica_groups=mesh['span'=8,'stream'=64] {'span','stream'}, use_global_device_ids=true, to_apply=%region_2.3 | all-reduce | flops 192 | bytes 1536 | tf_op jit(solution)/shard_map/psum | solution.py:156
  223.8 0.2 convolution_bitcast_fusion.3
  224.0 0.2 fusion
  224.2 0.2 fusion.61
  224.5 0.2 multiply_add_fusion
  224.9 0.2 copy-done.5
  225.1 0.6 fusion.62
  225.8 0.6 fusion.63
  226.5 1.9 fusion.10
  228.5 1.7 copy.49
  230.3 110.2 %reduce-scatter.2.cloned.1.call-done = f32[2,9,8,256]{3,2,1,0:T(8,128)} async-done(((f32[16,9,8,256]{3,2,1,0:T(8,128)}), f32[2,9,8,256]{3,2,1,0:T(8,128)}) %reduce-scatter.2.cloned.1.call-update) | async-done | bytes 147472 | tf_op jit(solution)/shard_map/reduce_scatter | solution.py:115
  340.5 0.9 fusion.59
  341.4 0.1 slice_add_fusion.1
  341.5 2.2 scatter-add.6
  343.7 0.1 slice_add_fusion
  343.8 2.2 scatter-add.9
  346.0 0.7 convolution_bitcast_fusion.1
  346.7 0.1 fusion.57
  346.8 12.4 %collective-permute-start.2 = (f32[9,1,8,256]{3,1,2,0:T(1,128)S(1)}, f32[9,1,8,256]{3,1,2,0:T(1,128)S(1)}, u32[]{:S(2)}, u32[]{:S(2)}) collective-permute-start(f32[9,1,8,256]{3,1,2,0:T(1,128)S(1)} %get-tuple-element.56), channel_id=1, source_target_pairs={{64,0},{128,64},{192,128},{256,192},{320,256},{384,320},{448,384},... | collective-permute-start | bytes 221192 | tf_op jit(solution)/shard_map/ppermute | solution.py:26
  359.2 1.9 collective-permute-start.3
  361.1 0.7 copy.53
  361.8 0.4 collective-permute-done.2
  362.2 15.2 %collective-permute-done.3 = f32[9,1,8,256]{3,1,2,0:T(1,128)S(1)} collective-permute-done((f32[9,1,8,256]{3,1,2,0:T(1,128)S(1)}, f32[9,1,8,256]{3,1,2,0:T(1,128)S(1)}, u32[]{:S(2)}, u32[]{:S(2)}) %collective-permute-start.3) | collective-permute-done | bytes 73760 | tf_op jit(solution)/shard_map/ppermute | solution.py:25
  377.4 0.3 fusion.7
  377.9 0.7 copy.54
  (53 shorter events, 1.2 us)
Async XLA Ops:
  8.9 33.1 %copy-start.2 = (f32[4,4,1,1]{1,0,3,2:T(4,128)S(1)}, f32[4,4,1,1]{1,0,3,2:T(4,128)}, u32[]{:S(2)}) copy-start(f32[4,4,1,1]{1,0,3,2:T(4,128)} %constant.110) | copy-start | bytes 196
  10.3 15.4 %collective-permute-start = (f32[10,1,8,256]{3,2,1,0:T(8,128)S(1)}, f32[10,1,8,256]{3,2,1,0:T(8,128)S(1)}, u32[]{:S(2)}, u32[]{:S(2)}) collective-permute-start(f32[10,1,8,256]{3,2,1,0:T(8,128)S(1)} %get-tuple-element.54), channel_id=1, source_target_pairs={{64,0},{128,64},{192,128},{256,192},{320,256},{384,320},{448,384},... | collective-permute-start | bytes 245768 | tf_op jit(solution)/shard_map/ppermute | solution.py:26
  23.7 18.2 %collective-permute-start.1 = (f32[10,1,8,256]{3,2,1,0:T(8,128)S(1)}, f32[10,1,8,256]{3,2,1,0:T(8,128)S(1)}, u32[]{:S(2)}, u32[]{:S(2)}) collective-permute-start(f32[10,1,8,256]{3,2,1,0:T(8,128)S(1)} %get-tuple-element.55), channel_id=1, source_target_pairs={{0,64},{64,128},{128,192},{192,256},{256,320},{320,384},{384,448},... | collective-permute-start | bytes 245768 | tf_op jit(solution)/shard_map/ppermute | solution.py:25
  44.7 57.4 %all-to-all-start = ((f32[8,2,10,8,256]{4,1,3,2,0:T(2,128)}), f32[8,2,10,8,256]{4,1,3,2,0:T(2,128)S(1)}, u32[]{:S(2)}, u32[]{:S(2)}) async-start(f32[8,2,10,8,256]{4,1,3,2,0:T(2,128)} %stack.17), calls=%async_computation | async-start | bytes 2621440 | tf_op jit(solution)/shard_map/all_to_all | solution.py:89
  49.0 291.4 %reduce-scatter.2.cloned.1.call-start = ((), (), s32[]{:S(2)}) async-start(), calls=%async_computation.2 | async-start | bytes 1327104 | tf_op jit(solution)/shard_map/reduce_scatter | solution.py:115
  103.7 1.7 copy-start.6
  103.7 1.7 copy-start.7
  105.2 0.9 copy-start
  105.2 1.0 copy-start.1
  105.2 1.0 copy-start.3
  105.4 1.2 copy-start.8
  224.5 0.7 copy-start.5
  224.7 1.1 copy-start.4
  346.8 15.4 %collective-permute-start.2 = (f32[9,1,8,256]{3,1,2,0:T(1,128)S(1)}, f32[9,1,8,256]{3,1,2,0:T(1,128)S(1)}, u32[]{:S(2)}, u32[]{:S(2)}) collective-permute-start(f32[9,1,8,256]{3,1,2,0:T(1,128)S(1)} %get-tuple-element.56), channel_id=1, source_target_pairs={{64,0},{128,64},{192,128},{256,192},{320,256},{384,320},{448,384},... | collective-permute-start | bytes 221192 | tf_op jit(solution)/shard_map/ppermute | solution.py:26
  359.2 18.2 %collective-permute-start.3 = (f32[9,1,8,256]{3,1,2,0:T(1,128)S(1)}, f32[9,1,8,256]{3,1,2,0:T(1,128)S(1)}, u32[]{:S(2)}, u32[]{:S(2)}) collective-permute-start(f32[9,1,8,256]{3,1,2,0:T(1,128)S(1)} %get-tuple-element.57), channel_id=1, source_target_pairs={{0,64},{64,128},{128,192},{192,256},{256,320},{320,384},{384,448},... | collective-permute-start | bytes 221192 | tf_op jit(solution)/shard_map/ppermute | solution.py:25
Sparse Core Ops, SparseCore 0:
  230.4 110.0 reduce-scatter.1
